TPU v7x, 32 devices: a whole 2x2x4 slice. The times are simulated.
32 devices in a mesh: seq: 8 (over y, x, core), head: 4 (over z).
Axes of the slice: x: 2, y: 2, z: 4, core: 2. Of those that a mesh axis runs over, the one named last changes fastest.
Arguments:
- activations: bfloat16 [4096, 5376], P(('seq', 'head')), may hold values from -42 to 42, as said below
- input_gain: float32 [5376], replicated, may hold values from 0.1 to 1.9
- query_weight: bfloat16 [5376, 4096], P(None, 'head'), may hold values from -2.2818633 to 2.2818633
- key_weight: bfloat16 [5376, 2048], P(None, 'head'), may hold values from -1 to 1
- value_weight: bfloat16 [5376, 2048], P(None, 'head'), may hold values from -0.078125 to 0.078125
- output_weight: bfloat16 [4096, 5376], P('head'), may hold values from -0.09375 to 0.09375
- cache_edge: bfloat16 [2, 1024, 2048], P(None, None, 'head'), may hold values from -6 to 6
- post_gain: float32 [5376], replicated, may hold values from 0.1 to 1.9
Outputs:
- layer_out: bfloat16 [4096, 5376], P(('seq', 'head'))
Inputs may be any that keep to these rules, and one draw needn't show every extreme that they name: `activations`: input rows with row and feature scales.
All inputs are finite; a program needn't handle non-finite values.
Results may differ from a plain program's by a relative error of at most 0.006.
Values may be sent and summed in bfloat16 or wider, within the bound.
A program may use at most 128 MiB of HBM per device.

v0:
```python
import jax
import jax.numpy as jnp
from jax import lax
from jax.sharding import PartitionSpec as P

HD = 128
WINDOW = 1024
SCALAR = 168
TOK_DEV = 512
EPSILON = 1e-06
ROPE_BASE = 10000.0


def from_behind(array, axis, by):
    count = lax.axis_size(axis)
    pairs = [(i, i + by) for i in range(count) if 0 <= i + by < count]
    return lax.ppermute(array, axis, pairs)


def normalize_rows(values, gain):
    return values * lax.rsqrt(jnp.mean(values * values, axis=-1, keepdims=True) + EPSILON) * gain


def rotate(vectors, positions):
    half_size = vectors.shape[-1] // 2
    frequency = ROPE_BASE ** (-(jnp.arange(half_size, dtype=jnp.float32) * 2.0 / vectors.shape[-1]))
    angles = positions[:, None] * frequency[None, :]
    cosine = jnp.cos(angles)[:, None, :]
    sine_part = jnp.sin(angles)[:, None, :]
    first_half = vectors[..., :half_size]
    second_half = vectors[..., half_size:]
    return jnp.concatenate(
        [
            first_half * cosine - second_half * sine_part,
            second_half * cosine + first_half * sine_part,
        ],
        axis=-1,
    )


def per_device(
    activations,
    input_gain,
    query_weight,
    key_weight,
    value_weight,
    output_weight,
    cache_edge,
    post_gain,
):
    heads_query = query_weight.shape[1] // HD
    heads_kv = key_weight.shape[1] // HD
    group_size = heads_query // heads_kv
    query_width = heads_query * HD
    kv_width = heads_kv * HD
    seq_pos = lax.axis_index("seq")
    first_pos = seq_pos * TOK_DEV
    normed = normalize_rows(activations.astype(jnp.float32), input_gain).astype(jnp.bfloat16)
    normed = lax.all_gather(normed, "head", axis=0, tiled=True)
    row_count = normed.shape[0]
    positions = (first_pos + jnp.arange(row_count, dtype=jnp.int32)).astype(jnp.float32)
    queries_raw = jnp.dot(normed, query_weight, preferred_element_type=jnp.float32)
    keys_raw = jnp.dot(normed, key_weight, preferred_element_type=jnp.float32)
    value_rows = jnp.dot(normed, value_weight, preferred_element_type=jnp.float32)
    queries = rotate(queries_raw.reshape(row_count, heads_query, HD), positions) * SCALAR ** (-0.5)
    keys = rotate(keys_raw.reshape(row_count, heads_kv, HD), positions)
    joined = jnp.concatenate(
        [queries.reshape(row_count, query_width), keys.reshape(row_count, kv_width), value_rows],
        axis=1,
    )
    packed = joined.astype(jnp.bfloat16)
    queries = packed[:, :query_width]
    own_edge = packed[:, query_width:]
    cache_rows = jnp.concatenate([cache_edge[0], cache_edge[1]], axis=1)
    reach_steps = WINDOW // TOK_DEV
    earlier = []
    received = own_edge
    for distance in range(1, reach_steps + 1):
        received = from_behind(own_edge, "seq", distance)
        offset = jnp.clip(WINDOW + (seq_pos - distance) * TOK_DEV, 0, WINDOW - TOK_DEV)
        from_cache = lax.dynamic_slice_in_dim(cache_rows, offset, TOK_DEV, 0)
        earlier.append(jnp.where(seq_pos >= distance, received, from_cache))
    window_rows = jnp.concatenate(earlier[::-1] + [own_edge], axis=0)
    span_length = window_rows.shape[0]
    key_rows = window_rows[:, :kv_width].reshape(span_length, heads_kv, HD)
    value_block = window_rows[:, kv_width:].reshape(span_length, heads_kv, HD)
    query_block = queries.reshape(TOK_DEV, heads_kv, group_size, HD)
    query_index = jnp.arange(TOK_DEV, dtype=jnp.int32)
    key_index = jnp.arange(span_length, dtype=jnp.int32)
    allowed = (key_index[None, :] > query_index[:, None]) & (
        key_index[None, :] <= query_index[:, None] + WINDOW
    )
    scores = jnp.einsum("qgrd,kgd->grqk", query_block, key_rows, preferred_element_type=jnp.float32)
    scores = jnp.where(allowed[None, None], scores, -jnp.inf)
    largest = jnp.max(scores, axis=-1, keepdims=True)
    exps = jnp.exp(scores - largest)
    probabilities = (exps / jnp.sum(exps, axis=-1, keepdims=True)).astype(jnp.bfloat16)
    attended = jnp.einsum(
        "grqk,kgd->qgrd", probabilities, value_block, preferred_element_type=jnp.float32
    )
    attended = attended.astype(jnp.bfloat16).reshape(TOK_DEV, query_width)
    projected = lax.psum_scatter(
        jnp.dot(attended, output_weight, preferred_element_type=jnp.float32).astype(jnp.bfloat16),
        "head",
        scatter_dimension=0,
        tiled=True,
    ).astype(jnp.float32)
    branch = normalize_rows(projected, post_gain)
    return (activations.astype(jnp.float32) + branch).astype(jnp.bfloat16)


def solution(mesh):
    return jax.shard_map(
        per_device,
        mesh=mesh,
        in_specs=(
            P(("seq", "head"), None),
            P(),
            P(None, "head"),
            P(None, "head"),
            P(None, "head"),
            P("head", None),
            P(None, None, "head"),
            P(),
        ),
        out_specs=P(("seq", "head"), None),
        check_vma=False,
    )
```

profile of v0, /device:TPU:0, one launch (start us, length us, event | category | flops | bytes accessed | tf_op | source)
XLA Modules:
  0.0 335.1 jit_solution(6270335785261173082)
XLA Ops:
  6.5 1.7 fusion.10
  8.2 2.8 fusion.12
  11.7 0.8 copy.11
  12.5 0.8 copy.12
  13.4 1.7 fusion.24
  16.1 1.5 fusion.7
  17.6 98.7 %all-gather.2.cloned.1.call-done = bf16[512,5376]{1,0:T(8,128)(2,1)} async-done(((bf16[128,5376]{1,0:T(8,128)(2,1)}), bf16[512,5376]{1,0:T(8,128)(2,1)}) %all-gather.2.cloned.1.call-update) | async-done | bytes 5505040 | tf_op jit(solution)/shard_map/all_gather | solution.py:59
  116.3 7.3 %fusion.26 = f32[512,512]{0,1:T(8,128)S(1)} fusion(bf16[512,5376]{1,0:T(8,128)(2,1)} %all-gather.2.cloned.1.call-done, bf16[5376,512]{1,0:T(8,128)(2,1)} %param.11), kind=kOutput, calls=%fused_computation.56 | convolution fusion | flops 2818572288 | bytes 12058624 | tf_op jit(solution)/shard_map/dot_general | solution.py:63
  123.9 5.8 %convolution_convert_fusion.1 = bf16[512,512]{0,1:T(8,128)(2,1)S(1)} fusion(bf16[512,5376]{1,0:T(8,128)(2,1)S(1)} %copy-done.4, bf16[5376,512]{1,0:T(8,128)(2,1)} %param.12), kind=kOutput, calls=%fused_computation.35 | convolution fusion | flops 2818834432 | bytes 11534336 | tf_op jit(solution)/shard_map/dot_general | solution.py:64
  129.8 2.0 collective-permute-start.1
  131.8 3.8 %collective-permute-start = (bf16[512,1024]{0,1:T(8,128)(2,1)S(1)}, bf16[512,1024]{0,1:T(8,128)(2,1)S(1)}, u32[]{:S(2)}, u32[]{:S(2)}) collective-permute-start(bf16[512,1024]{0,1:T(8,128)(2,1)S(1)} %pad_maximum_fusion), channel_id=1, source_target_pairs={{0,8},{4,12},{8,16},{12,20},{16,24},{20,28},{1,9},{5,13},{9,17},{1... | collective-permute-start | bytes 3145736 | tf_op jit(solution)/shard_map/ppermute | solution.py:17
  135.7 5.8 %convolution_bitcast_fusion = f32[64,8,8,128]{3,1,2,0:T(8,128)S(1)} fusion(bf16[512,5376]{1,0:T(8,128)(2,1)S(1)} %copy-done.4, bf16[5376,1024]{1,0:T(8,128)(2,1)S(1)} %bitcast.59), kind=kOutput, calls=%fused_computation.33 | convolution fusion | flops 5637144576 | bytes 18612224 | tf_op jit(solution)/shard_map/dot_general | solution.py:62
  142.5 1.1 multiply_subtract_fusion
  144.4 14.3 %collective-permute-done = bf16[512,1024]{0,1:T(8,128)(2,1)S(1)} collective-permute-done((bf16[512,1024]{0,1:T(8,128)(2,1)S(1)}, bf16[512,1024]{0,1:T(8,128)(2,1)S(1)}, u32[]{:S(2)}, u32[]{:S(2)}) %collective-permute-start) | collective-permute-done | bytes 1048608 | tf_op jit(solution)/shard_map/ppermute | solution.py:17
  158.7 2.2 fusion.19
  160.9 9.5 %maximum_maximum_fusion = bf16[1536,1024]{0,1:T(8,128)(2,1)S(1)} fusion(bf16[512,512]{0,1:T(8,128)(2,1)S(1)} %convolution_convert_fusion.1, bf16[512,512]{0,1:T(8,128)(2,1)S(1)} %bitcast.51, bf16[512,1024]{0,1:T(8,128)(2,1)S(1)} %get-tuple-element.10, bf16[512,1024]{0,1:T(8,128)(2,1)S(1)} %get-tuple-element.9), kind=kLoop, calls=%fused_computation.15 | loop fusion | flops 12582912 | bytes 6291456 | tf_op jit(solution)/shard_map/concatenate | solution.py:83
  170.4 1.4 fusion.23
  171.8 11.8 %fusion.27 = f32[4,1536,512,2]{2,1,3,0:T(8,128)} fusion(bf16[1536,4,128,1]{0,2,3,1:T(8,128)(2,1)S(1)} %bitcast.48, bf16[512,4,2,128]{3,0,2,1:T(8,128)(2,1)S(1)} %bitcast.54), kind=kOutput, calls=%fused_computation.57 | convolution fusion | flops 1610612736 | bytes 27787264 | tf_op jit(solution)/shard_map/qgrd,kgd->grqk/dot_general | solution.py:93
  183.6 9.2 %fusion.25 = f32[4,2,512]{2,1,0:T(2,128)S(1)} fusion(pred[512,1536]{0,1:T(8,128)(4,1)} %fusion.7, bf16[1536,4,128,1]{0,2,3,1:T(8,128)(2,1)S(1)} %bitcast.49, bf16[512,4,2,128]{3,0,2,1:T(8,128)(2,1)S(1)} %bitcast.55), kind=kOutput, calls=%fused_computation.55 | convolution fusion | flops 1629488640 | bytes 3424256 | tf_op jit(solution)/shard_map/sub | solution.py:96
  192.8 13.0 %fusion.15 = bf16[4,128,2,512]{3,1,2,0:T(8,128)(2,1)S(1)} fusion(bf16[1536,4,128,1]{0,2,3,1:T(8,128)(2,1)} %bitcast.56, f32[4,2,512]{2,1,0:T(2,128)S(1)} %fusion.25, f32[4,1536,512,2]{2,1,3,0:T(8,128)} %fusion.27, pred[512,1536]{0,1:T(8,128)(4,1)} %fusion.7), kind=kOutput, calls=%fused_computation.34 | convolution fusion | flops 1636308480 | bytes 28590080 | tf_op jit(solution)/shard_map/grqk,kgd->qgrd/dot_general | solution.py:98
  205.8 11.9 %convolution_convert_fusion = bf16[512,5376]{1,0:T(8,128)(2,1)} fusion(bf16[512,1024]{0,1:T(8,128)(2,1)S(1)} %bitcast.60, bf16[1024,5376]{1,0:T(8,128)(2,1)} %param.13), kind=kOutput, calls=%fused_computation.8 | convolution fusion | flops 5639897088 | bytes 17563648 | tf_op jit(solution)/shard_map/dot_general | solution.py:103
  217.7 105.6 %reduce-scatter.2.cloned.1.call-done = bf16[128,5376]{1,0:T(8,128)(2,1)} async-done(((bf16[512,5376]{1,0:T(8,128)(2,1)}), bf16[128,5376]{1,0:T(8,128)(2,1)}) %reduce-scatter.2.cloned.1.call-update) | async-done | bytes 1376272 | tf_op jit(solution)/shard_map/reduce_scatter | solution.py:102
  323.3 1.7 fusion.8
  325.0 3.0 fusion.13
  (36 shorter events, 3.8 us)
Async XLA Ops:
  6.5 109.8 %all-gather.2.cloned.1.call-start = ((), (), s32[]{:S(2)}) async-start(), calls=%async_computation.1 | async-start | bytes 6881280 | tf_op jit(solution)/shard_map/all_gather | solution.py:59
  11.1 312.2 %reduce-scatter.2.cloned.1.call-start = ((), (), s32[]{:S(2)}) async-start(), calls=%async_computation.2 | async-start | bytes 6881280 | tf_op jit(solution)/shard_map/reduce_scatter | solution.py:102
  116.3 7.6 %copy-start.4 = (bf16[512,5376]{1,0:T(8,128)(2,1)S(1)}, bf16[512,5376]{1,0:T(8,128)(2,1)}, u32[]{:S(2)}) copy-start(bf16[512,5376]{1,0:T(8,128)(2,1)} %all-gather.2.cloned.1.call-done) | copy-start | bytes 16515076
  123.8 11.8 %slice-start = ((s8[11010048]{0:T(1024)(128)(4,1)}), s8[4194304]{0:T(1024)(128)(4,1)S(1)}, s32[]{:S(2)}) async-start(s8[11010048]{0:T(1024)(128)(4,1)} %bitcast.58), calls=%async_computation.3 | async-start | bytes 8388608
  123.9 11.7 %slice-start.1 = ((s8[11010048]{0:T(1024)(128)(4,1)}), s8[4194304]{0:T(1024)(128)(4,1)S(1)}, s32[]{:S(2)}) async-start(s8[11010048]{0:T(1024)(128)(4,1)} %bitcast.58), calls=%async_computation.4 | async-start | bytes 8388608
  123.9 11.7 %slice-start.2 = ((s8[11010048]{0:T(1024)(128)(4,1)}), s8[2621440]{0:T(1024)(128)(4,1)S(1)}, s32[]{:S(2)}) async-start(s8[11010048]{0:T(1024)(128)(4,1)} %bitcast.58), calls=%async_computation.5 | async-start | bytes 5242880
  129.8 14.6 %collective-permute-start.1 = (bf16[512,1024]{0,1:T(8,128)(2,1)S(1)}, bf16[512,1024]{0,1:T(8,128)(2,1)S(1)}, u32[]{:S(2)}, u32[]{:S(2)}) collective-permute-start(bf16[512,1024]{0,1:T(8,128)(2,1)S(1)} %pad_maximum_fusion), channel_id=1, source_target_pairs={{0,4},{4,8},{8,12},{12,16},{16,20},{20,24},{24,28},{1,5},{5,9},{9,... | collective-permute-start | bytes 3145736 | tf_op jit(solution)/shard_map/ppermute | solution.py:17
  131.8 26.9 %collective-permute-start = (bf16[512,1024]{0,1:T(8,128)(2,1)S(1)}, bf16[512,1024]{0,1:T(8,128)(2,1)S(1)}, u32[]{:S(2)}, u32[]{:S(2)}) collective-permute-start(bf16[512,1024]{0,1:T(8,128)(2,1)S(1)} %pad_maximum_fusion), channel_id=1, source_target_pairs={{0,8},{4,12},{8,16},{12,20},{16,24},{20,28},{1,9},{5,13},{9,17},{1... | collective-permute-start | bytes 3145736 | tf_op jit(solution)/shard_map/ppermute | solution.py:17
  141.5 1.0 copy-start.1
  141.5 1.0 copy-start.2
  217.6 107.4 %copy-start = (bf16[128,5376]{1,0:T(8,128)(2,1)S(1)}, bf16[128,5376]{1,0:T(8,128)(2,1)}, u32[]{:S(2)}) copy-start(bf16[128,5376]{1,0:T(8,128)(2,1)} %param.8) | copy-start | bytes 4128772
  217.6 107.4 %copy-start.3 = (f32[5376]{0:T(1024)S(1)}, f32[5376]{0:T(1024)}, u32[]{:S(2)}) copy-start(f32[5376]{0:T(1024)} %param.15) | copy-start | bytes 64516
Sparse Core Ops, SparseCore 0:
  11.2 105.0 all-gather.1
  217.8 105.4 reduce-scatter.1
where the time goes:
time: 341 us; the launch traced here: 335 us
  waiting for transfers between devices  219 us (64%)
  matrix products  64.7 us (19%)
  other arithmetic  24.8 us (7%)
  between operations  13.9 us (4%)
  local copies, waits for them, and re-layouts  7 us (2%)
  starting transfers between devices  5.89 us (2%)
    reduce_scatter x1, waiting for transfers between devices, per_device(): lax.psum_scatter(jnp.dot(attended, output_weight, preferred_element_type=...  106 us
    all_gather x1, waiting for transfers between devices, per_device(): normed = lax.all_gather(normed, 'head', axis=0, tiled=True)  98.7 us
    ppermute x2, waiting for transfers between devices, from_behind(): return lax.ppermute(array, axis, pairs)  14.3 us
    dot_general x1, matrix products, per_device(): jnp.einsum('grqk,kgd->qgrd', probabilities, value_block, preferred_elemen...  13 us
    dot_general x1, matrix products, per_device(): jnp.dot(attended, output_weight, preferred_element_type=jnp.float32)  11.9 us
    dot_general x1, matrix products, per_device(): jnp.einsum('qgrd,kgd->grqk', query_block, key_rows, preferred_element_typ...  11.8 us
    concatenate x1, other arithmetic, per_device(): window_rows = jnp.concatenate(earlier[::-1] + [own_edge], axis=0)  9.49 us
    sub x1, matrix products, per_device(): exps = jnp.exp(scores - largest)  9.22 us
  transfers between devices with their start and end apart: 4, of which 3 were waited for; matrix products, arithmetic and copies ran while one was open for 4% of the time, Pallas kernels for 0%

commit v1 on v0

--- a/solution.py
+++ b/solution.py
@@ -9,6 +9,16 @@
 TOK_DEV = 512
 EPSILON = 1e-06
 ROPE_BASE = 10000.0
+
+
+def pass_along(block, axis, dim):
+    size = lax.axis_size(axis)
+    current, blocks = (block, [block])
+    for _ in range(size - 1):
+        current = lax.ppermute(current, axis, [(i, (i + 1) % size) for i in range(size)])
+        blocks.insert(0, current)
+    line = jnp.concatenate(blocks, axis=dim)
+    return jnp.roll(line, (lax.axis_index(axis) + 1) * block.shape[dim], axis=dim)
 
 
 def from_behind(array, axis, by):
@@ -56,7 +66,7 @@
     seq_pos = lax.axis_index("seq")
     first_pos = seq_pos * TOK_DEV
     normed = normalize_rows(activations.astype(jnp.float32), input_gain).astype(jnp.bfloat16)
-    normed = lax.all_gather(normed, "head", axis=0, tiled=True)
+    normed = pass_along(normed, "head", 0)
     row_count = normed.shape[0]
     positions = (first_pos + jnp.arange(row_count, dtype=jnp.int32)).astype(jnp.float32)
     queries_raw = jnp.dot(normed, query_weight, preferred_element_type=jnp.float32)

time: 341 us -> 332 us (0.974); the launches traced: 335 us -> 332 us
  waiting for transfers between devices: 219 us -> 206 us
  local copies, waits for them, and re-layouts: 7 us -> 14.2 us
    all_gather x1 -> x0, waiting for transfers between devices: 98.7 us -> none  [per_device(): normed = lax.all_gather(normed, 'head', axis=0, tiled=True)]
    ppermute x0 -> x3, waiting for transfers between devices: none -> 87.9 us  [pass_along(): lax.ppermute(current, axis, [(i, (i + 1) % size) for i in range(size)])]
    unnamed x19 -> x25, local copies, waits for them, and re-layouts: 2.11 us -> 9.39 us
  transfers between devices with their start and end apart: 4 -> 6, of which waited for: 3 -> 5; matrix products, arithmetic and copies ran while one was open for 4% -> 6% of each run, Pallas kernels for 0% -> 0%
where the time goes in v1:
time: 332 us
  waiting for transfers between devices  206 us (62%)
  matrix products  65.4 us (20%)
  other arithmetic  24.6 us (7%)
  local copies, waits for them, and re-layouts  14.2 us (4%)
  between operations  13.7 us (4%)
  starting transfers between devices  8.15 us (2%)
    reduce_scatter x1, waiting for transfers between devices, per_device(): lax.psum_scatter(jnp.dot(attended, output_weight, preferred_element_type=...  105 us
    ppermute x3, waiting for transfers between devices, pass_along(): lax.ppermute(current, axis, [(i, (i + 1) % size) for i in range(size)])  87.9 us
    dot_general x1, matrix products, per_device(): jnp.einsum('grqk,kgd->qgrd', probabilities, value_block, preferred_elemen...  13 us
    ppermute x2, waiting for transfers between devices, from_behind(): return lax.ppermute(array, axis, pairs)  12.4 us
    dot_general x1, matrix products, per_device(): jnp.dot(attended, output_weight, preferred_element_type=jnp.float32)  12.1 us
    dot_general x1, matrix products, per_device(): jnp.einsum('qgrd,kgd->grqk', query_block, key_rows, preferred_element_typ...  11.8 us
    concatenate x1, other arithmetic, per_device(): window_rows = jnp.concatenate(earlier[::-1] + [own_edge], axis=0)  9.52 us
    unnamed x25, local copies, waits for them, and re-layouts  9.39 us
  transfers between devices with their start and end apart: 6, of which 5 were waited for; matrix products, arithmetic and copies ran while one was open for 6% of the time, Pallas kernels for 0%

profile of v1, /device:TPU:0, one launch (start us, length us, event | category | flops | bytes accessed | tf_op | source)
XLA Modules:
  0.0 331.7 jit_solution(16539235749469659145)
XLA Ops:
  6.5 1.7 fusion.16
  8.2 1.7 fusion.18
  10.0 3.1 collective-permute-start
  13.0 32.2 %collective-permute-done = bf16[128,5376]{1,0:T(8,128)(2,1)S(1)} collective-permute-done((bf16[128,5376]{1,0:T(8,128)(2,1)S(1)}, bf16[128,5376]{1,0:T(8,128)(2,1)S(1)}, u32[]{:S(2)}, u32[]{:S(2)}) %collective-permute-start) | collective-permute-done | bytes 1376288 | tf_op jit(solution)/shard_map/ppermute | solution.py:18
  45.3 33.2 %collective-permute-done.1 = bf16[128,5376]{1,0:T(8,128)(2,1)S(1)} collective-permute-done((bf16[128,5376]{1,0:T(8,128)(2,1)S(1)}, bf16[128,5376]{1,0:T(8,128)(2,1)S(1)}, u32[]{:S(2)}, u32[]{:S(2)}) %collective-permute-start.1) | collective-permute-done | bytes 1376288 | tf_op jit(solution)/shard_map/ppermute | solution.py:18
  79.3 3.0 fusion.39
  82.2 2.3 copy.22
  84.5 2.3 copy.21
  86.8 1.5 fusion.13
  88.3 22.5 %collective-permute-done.2 = bf16[128,5376]{1,0:T(8,128)(2,1)} collective-permute-done((bf16[128,5376]{1,0:T(8,128)(2,1)S(1)}, bf16[128,5376]{1,0:T(8,128)(2,1)}, u32[]{:S(2)}, u32[]{:S(2)}) %collective-permute-start.2) | collective-permute-done | bytes 1376288 | tf_op jit(solution)/shard_map/ppermute | solution.py:18
  116.0 5.6 %fusion.25 = bf16[512,512]{0,1:T(8,128)(2,1)S(1)} fusion(bf16[5376,512]{1,0:T(8,128)(2,1)} %param.12, bf16[1024,5376]{1,0:T(8,128)(2,1)S(1)} %constant_dynamic-update-slice_fusion, s32[]{:T(128)S(6)} %select_n.35), kind=kOutput, calls=%fused_computation.41 | convolution fusion | flops 2818834432 | bytes 11534340 | tf_op jit(solution)/shard_map/dot_general | solution.py:74
  121.6 5.1 %fusion.11 = f32[512,512]{0,1:T(8,128)S(1)} fusion(bf16[5376,512]{1,0:T(8,128)(2,1)} %param.11, bf16[1024,5376]{1,0:T(8,128)(2,1)S(1)} %constant_dynamic-update-slice_fusion, s32[]{:T(128)S(6)} %select_n.35), kind=kOutput, calls=%fused_computation.14 | convolution fusion | flops 2818572288 | bytes 12058628 | tf_op jit(solution)/shard_map/dot_general | solution.py:73
  128.4 3.7 %collective-permute-start.3 = (bf16[512,1024]{0,1:T(8,128)(2,1)S(1)}, bf16[512,1024]{0,1:T(8,128)(2,1)S(1)}, u32[]{:S(2)}, u32[]{:S(2)}) collective-permute-start(bf16[512,1024]{0,1:T(8,128)(2,1)S(1)} %pad_maximum_fusion), channel_id=1, source_target_pairs={{0,8},{4,12},{8,16},{12,20},{16,24},{20,28},{1,9},{5,13},{9,17},{1... | collective-permute-start | bytes 3145736 | tf_op jit(solution)/shard_map/ppermute | solution.py:27
  132.1 8.6 %fusion.21 = f32[64,8,8,128]{3,1,2,0:T(8,128)S(1)} fusion(bf16[5376,1024]{1,0:T(8,128)(2,1)} %param.10, bf16[1024,5376]{1,0:T(8,128)(2,1)S(1)} %constant_dynamic-update-slice_fusion, s32[]{:T(128)S(6)} %select_n.35), kind=kOutput, calls=%fused_computation.39 | convolution fusion | flops 5637144576 | bytes 18612228 | tf_op jit(solution)/shard_map/dot_general | solution.py:72
  143.1 12.4 %collective-permute-done.3 = bf16[512,1024]{0,1:T(8,128)(2,1)S(1)} collective-permute-done((bf16[512,1024]{0,1:T(8,128)(2,1)S(1)}, bf16[512,1024]{0,1:T(8,128)(2,1)S(1)}, u32[]{:S(2)}, u32[]{:S(2)}) %collective-permute-start.3) | collective-permute-done | bytes 1048608 | tf_op jit(solution)/shard_map/ppermute | solution.py:27
  155.4 2.2 fusion.31
  157.6 9.5 %maximum_maximum_fusion = bf16[1536,1024]{0,1:T(8,128)(2,1)S(1)} fusion(bf16[512,512]{0,1:T(8,128)(2,1)S(1)} %fusion.25, bf16[512,512]{0,1:T(8,128)(2,1)S(1)} %bitcast.48, bf16[512,1024]{0,1:T(8,128)(2,1)S(1)} %get-tuple-element.10, bf16[512,1024]{0,1:T(8,128)(2,1)S(1)} %get-tuple-element.9), kind=kLoop, calls=%fused_computation.21 | loop fusion | flops 12582912 | bytes 6291456 | tf_op jit(solution)/shard_map/concatenate | solution.py:93
  168.6 11.8 %fusion.41 = f32[4,1536,512,2]{2,1,3,0:T(8,128)} fusion(bf16[1536,4,128,1]{0,2,3,1:T(8,128)(2,1)S(1)} %bitcast.45, bf16[512,4,2,128]{3,0,2,1:T(8,128)(2,1)S(1)} %bitcast.51), kind=kOutput, calls=%fused_computation.73 | convolution fusion | flops 1610612736 | bytes 27787264 | tf_op jit(solution)/shard_map/qgrd,kgd->grqk/dot_general | solution.py:103
  180.4 9.2 %fusion.40 = f32[4,2,512]{2,1,0:T(2,128)S(1)} fusion(pred[512,1536]{0,1:T(8,128)(4,1)} %fusion.13, bf16[1536,4,128,1]{0,2,3,1:T(8,128)(2,1)S(1)} %bitcast.46, bf16[512,4,2,128]{3,0,2,1:T(8,128)(2,1)} %bitcast.52), kind=kOutput, calls=%fused_computation.72 | convolution fusion | flops 1629488640 | bytes 3424256 | tf_op jit(solution)/shard_map/sub | solution.py:106
  189.6 13.0 %fusion.24 = bf16[4,128,2,512]{3,1,2,0:T(8,128)(2,1)S(1)} fusion(bf16[1536,4,128,1]{0,2,3,1:T(8,128)(2,1)} %bitcast.53, f32[4,2,512]{2,1,0:T(2,128)S(1)} %fusion.40, f32[4,1536,512,2]{2,1,3,0:T(8,128)} %fusion.41, pred[512,1536]{0,1:T(8,128)(4,1)} %fusion.13), kind=kOutput, calls=%fused_computation.40 | convolution fusion | flops 1636308480 | bytes 28590080 | tf_op jit(solution)/shard_map/grqk,kgd->qgrd/dot_general | solution.py:108
  202.6 12.1 %convolution_convert_fusion = bf16[512,5376]{1,0:T(8,128)(2,1)} fusion(bf16[512,1024]{0,1:T(8,128)(2,1)S(1)} %bitcast.55, bf16[1024,5376]{1,0:T(8,128)(2,1)} %param.13), kind=kOutput, calls=%fused_computation.8 | convolution fusion | flops 5639897088 | bytes 17563648 | tf_op jit(solution)/shard_map/dot_general | solution.py:113
  214.7 105.5 %reduce-scatter.2.cloned.1.call-done = bf16[128,5376]{1,0:T(8,128)(2,1)} async-done(((bf16[512,5376]{1,0:T(8,128)(2,1)}), bf16[128,5376]{1,0:T(8,128)(2,1)}) %reduce-scatter.2.cloned.1.call-update) | async-done | bytes 1376272 | tf_op jit(solution)/shard_map/reduce_scatter | solution.py:112
  320.2 1.7 fusion.14
  321.9 3.0 fusion.19
  (46 shorter events, 11.4 us)
Async XLA Ops:
  6.5 313.7 %reduce-scatter.2.cloned.1.call-start = ((), (), s32[]{:S(2)}) async-start(), calls=%async_computation.1 | async-start | bytes 6881280 | tf_op jit(solution)/shard_map/reduce_scatter | solution.py:112
  10.0 35.3 %collective-permute-start = (bf16[128,5376]{1,0:T(8,128)(2,1)S(1)}, bf16[128,5376]{1,0:T(8,128)(2,1)S(1)}, u32[]{:S(2)}, u32[]{:S(2)}) collective-permute-start(bf16[128,5376]{1,0:T(8,128)(2,1)S(1)} %fusion.18), channel_id=1, source_target_pairs={{0,1},{1,2},{2,3},{3,0},{4,5},{5,6},{6,7},{7,4},{8,9},{9,10},{10,1... | collective-permute-start | bytes 4128776 | tf_op jit(solution)/shard_map/ppermute | solution.py:18
  45.3 33.2 %collective-permute-start.1 = (bf16[128,5376]{1,0:T(8,128)(2,1)S(1)}, bf16[128,5376]{1,0:T(8,128)(2,1)S(1)}, u32[]{:S(2)}, u32[]{:S(2)}) collective-permute-start(bf16[128,5376]{1,0:T(8,128)(2,1)S(1)} %collective-permute-done), channel_id=1, source_target_pairs={{0,1},{1,2},{2,3},{3,0},{4,5},{5,6},{6,7},{7,4},{8,9},{9,10},{10,1... | collective-permute-start | bytes 4128776 | tf_op jit(solution)/shard_map/ppermute | solution.py:18
  78.4 6.1 %copy-start.1 = (bf16[128,5376]{1,0:T(8,128)(2,1)}, bf16[128,5376]{1,0:T(8,128)(2,1)S(1)}, u32[]{:S(2)}) copy-start(bf16[128,5376]{1,0:T(8,128)(2,1)S(1)} %collective-permute-done.1) | copy-start | bytes 4128772
  78.4 32.3 %collective-permute-start.2 = (bf16[128,5376]{1,0:T(8,128)(2,1)S(1)}, bf16[128,5376]{1,0:T(8,128)(2,1)}, u32[]{:S(2)}, u32[]{:S(2)}) collective-permute-start(bf16[128,5376]{1,0:T(8,128)(2,1)S(1)} %collective-permute-done.1), channel_id=1, source_target_pairs={{0,1},{1,2},{2,3},{3,0},{4,5},{5,6},{6,7},{7,4},{8,9},{9,10},{10,1... | collective-permute-start | bytes 4128776 | tf_op jit(solution)/shard_map/ppermute | solution.py:18
  86.8 25.4 %copy-start.2 = (bf16[128,5376]{1,0:T(8,128)(2,1)S(1)}, bf16[128,5376]{1,0:T(8,128)(2,1)}, u32[]{:S(2)}) copy-start(bf16[128,5376]{1,0:T(8,128)(2,1)} %copy-done.1) | copy-start | bytes 4128772
  112.2 1.3 copy-start
  112.2 1.3 copy-start.6
  127.0 16.1 %collective-permute-start.4 = (bf16[512,1024]{0,1:T(8,128)(2,1)S(1)}, bf16[512,1024]{0,1:T(8,128)(2,1)S(1)}, u32[]{:S(2)}, u32[]{:S(2)}) collective-permute-start(bf16[512,1024]{0,1:T(8,128)(2,1)S(1)} %pad_maximum_fusion), channel_id=1, source_target_pairs={{0,4},{4,8},{8,12},{12,16},{16,20},{20,24},{24,28},{1,5},{5,9},{9,... | collective-permute-start | bytes 3145736 | tf_op jit(solution)/shard_map/ppermute | solution.py:27
  128.4 27.1 %collective-permute-start.3 = (bf16[512,1024]{0,1:T(8,128)(2,1)S(1)}, bf16[512,1024]{0,1:T(8,128)(2,1)S(1)}, u32[]{:S(2)}, u32[]{:S(2)}) collective-permute-start(bf16[512,1024]{0,1:T(8,128)(2,1)S(1)} %pad_maximum_fusion), channel_id=1, source_target_pairs={{0,8},{4,12},{8,16},{12,20},{16,24},{20,28},{1,9},{5,13},{9,17},{1... | collective-permute-start | bytes 3145736 | tf_op jit(solution)/shard_map/ppermute | solution.py:27
  142.3 13.2 %copy-start.3 = (bf16[1,1024,512]{1,2,0:T(8,128)(2,1)S(1)}, bf16[1,1024,512]{1,2,0:T(8,128)(2,1)}, u32[]{:S(2)}) copy-start(bf16[1,1024,512]{1,2,0:T(8,128)(2,1)} %copy.22) | copy-start | bytes 3145732
  142.3 13.2 %copy-start.4 = (bf16[1,1024,512]{1,2,0:T(8,128)(2,1)S(1)}, bf16[1,1024,512]{1,2,0:T(8,128)(2,1)}, u32[]{:S(2)}) copy-start(bf16[1,1024,512]{1,2,0:T(8,128)(2,1)} %copy.21) | copy-start | bytes 3145732
  143.1 25.5 %copy-start.5 = (bf16[512,8,128]{2,0,1:T(8,128)(2,1)}, bf16[512,8,128]{2,0,1:T(8,128)(2,1)S(1)}, u32[]{:S(2)}) copy-start(bf16[512,8,128]{2,0,1:T(8,128)(2,1)S(1)} %copy.13) | copy-start | bytes 3145732
  214.7 107.2 %copy-start.7 = (f32[5376]{0:T(1024)S(1)}, f32[5376]{0:T(1024)}, u32[]{:S(2)}) copy-start(f32[5376]{0:T(1024)} %param.15) | copy-start | bytes 64516
Sparse Core Ops, SparseCore 0:
  214.8 105.3 reduce-scatter.1
